TPU v7x, 128 devices: a whole 4x4x4 slice. The times are simulated.
128 devices in a mesh: scene: 8 (over y, core), seg: 16 (over x, z).
Axes of the slice: x: 4, y: 4, z: 4, core: 2. Of those that a mesh axis runs over, the one named last changes fastest.
Arguments:
- points: bfloat16 [196608, 512], P(('scene', 'seg')), may hold values from -6 to 6
- zorder: int32 [1536], P(('scene', 'seg')), may hold values from 0 to 1535, as said below
- image: bfloat16 [16384, 1024], P(('scene', 'seg')), may hold values from -6 to 6
- image_row: int32 [196608], P(('scene', 'seg')), may hold values from 0 to 16383, as said below
- image_weight: bfloat16 [1024, 512], replicated, may hold values from -0.1875 to 0.1875
- norm_gain: float32 [2, 2, 512], replicated, may hold values from 0.1 to 1.9
- in_weight: bfloat16 [2, 512, 1536], replicated, may hold values from -16 to 16
- out_weight: bfloat16 [2, 512, 512], replicated, may hold values from -0.25 to 0.25
- up_weight: bfloat16 [2, 512, 2048], replicated, may hold values from -0.25 to 0.25
- down_weight: bfloat16 [2, 2048, 512], replicated, may hold values from -0.125 to 0.125
- hilbert_target: int32 [1536], P(('scene', 'seg')), may hold values from 0 to 1535, as said below
Outputs:
- features: bfloat16 [196608, 512], P(('scene', 'seg'))
Inputs may be any that keep to these rules, and one draw needn't show every extreme that they name: zorder holds, for each device, a permutation of that device's 12 global block numbers. `image_row`: the row lies on a device of any scene group whose seg index equals that of the point's device. Within each scene group hilbert_target is a permutation of the group's block numbers; of one device's blocks at most 2 go to any one device, and in every draw some device hands exactly 2 blocks to another.
All inputs are finite; a program needn't handle non-finite values.
Results may differ from a plain program's by a relative error of at most 0.019.
Values may be sent and summed in bfloat16 or wider, within the bound.
A program may use at most 192 MiB of HBM per device.

v0:
```python
import functools

import jax
import jax.numpy as jnp
from jax import lax
from jax.experimental import pallas as pl
from jax.experimental.pallas import tpu as pltpu
from jax.sharding import PartitionSpec as P

HEAD_DIM = 16
PATCH = 512
EPS = 1e-05
LOG2E = 1.4426950408889634
MESH = pl.DeviceIdType.MESH
F32, BF16, I32 = jnp.float32, jnp.bfloat16, jnp.int32
NT = (((1,), (1,)), ((), ()))
ROWS, COLS = 16, 256
VMEM_LIMIT = 60 * 2**20


def mm(a, b):
    return jnp.dot(a, b, preferred_element_type=F32)


def image_kernel(n_scene, n_seg, blocks, image_ref, weight_ref, target_ref, table_ref, inverse_ref,
                 rows, columns, send, recv, fsend, frecv, tsend, trecv):
    scene = lax.axis_index("scene")
    seg = lax.axis_index("seg")
    core = scene % 2
    level = scene // 2
    chips = n_scene // 2
    other = level * 2 + 1 - core
    barrier = pltpu.get_barrier_semaphore()
    for k in range(1, chips):
        peer = (level + k) % chips * 2 + core
        pl.semaphore_signal(barrier, inc=1, device_id=(peer, seg), device_id_type=MESH)
    pl.semaphore_signal(barrier, inc=1, device_id=(other, seg), device_id_type=MESH)
    for k in range(1, n_seg):
        pl.semaphore_signal(barrier, inc=1, device_id=(scene, (seg + k) % n_seg), device_id_type=MESH)
    rows[scene] = mm(image_ref[...], weight_ref[...]).astype(BF16)
    columns[seg] = target_ref[...]
    pl.semaphore_wait(barrier, chips - 1 + 1 + n_seg - 1)

    def across(k):
        return pltpu.make_async_remote_copy(
            rows.at[scene], rows.at[scene], send.at[k], recv.at[k],
            device_id=((level + k) % chips * 2 + core, seg), device_id_type=MESH)

    def forward(k):
        held = (level + chips - k) % chips * 2 + core
        return pltpu.make_async_remote_copy(
            rows.at[held], rows.at[held], fsend.at[k], frecv.at[k],
            device_id=(other, seg), device_id_type=MESH)

    def targets(k):
        return pltpu.make_async_remote_copy(
            columns.at[seg], columns.at[seg], tsend.at[k], trecv.at[k],
            device_id=(scene, (seg + k) % n_seg), device_id_type=MESH)

    for k in (1, chips - 1, 2):
        across(k).start()
    forward(0).start()
    for k in range(1, n_seg):
        targets(k).start()
    for k in (1, chips - 1, 2):
        across(k).wait_recv()
        forward(k).start()
    for k in range(1, n_seg):
        targets(k).wait()
    base = scene * (n_seg * blocks)
    place = lax.broadcasted_iota(I32, (16, 128), 0)
    lane = lax.broadcasted_iota(I32, (16, 128), 1)
    within = place // 4 * (n_seg * 4) + place % 4
    for part in range(2):
        total = jnp.zeros((16, 128), I32)
        for source in range(n_seg):
            hit = columns[source] == lane + (base + part * 128)
            total = total + jnp.where(hit, within + source * 4, 0)
        summed = total[:8] + total[8:]
        for step in (4, 2, 1):
            summed = summed[:step] + summed[step:]
        inverse_ref[part:part + 1, :] = summed
    for k in range(chips):
        forward(k).wait_recv()
    for k in (1, chips - 1, 2):
        across(k).wait_send()
    for k in range(chips):
        forward(k).wait_send()
    table_ref[...] = rows[...].reshape(table_ref.shape)


def image_stage(image, weight, target, n_scene, n_seg):
    count, depth = image.shape
    width = weight.shape[1]
    blocks = target.shape[0]
    column = jnp.broadcast_to(jnp.pad(target, (0, 16 - blocks), constant_values=-1)[:, None], (16, 128))
    return pl.pallas_call(
        functools.partial(image_kernel, n_scene, n_seg, blocks),
        out_shape=(jax.ShapeDtypeStruct((n_scene * count, width), BF16), jax.ShapeDtypeStruct((2, 128), I32)),
        in_specs=[pl.BlockSpec(memory_space=pltpu.VMEM)] * 3,
        out_specs=(pl.BlockSpec(memory_space=pltpu.VMEM),) * 2,
        scratch_shapes=[
            pltpu.VMEM((n_scene, count, width), BF16),
            pltpu.VMEM((n_seg, 16, 128), I32),
            pltpu.SemaphoreType.DMA((n_scene // 2,)),
            pltpu.SemaphoreType.DMA((n_scene // 2,)),
            pltpu.SemaphoreType.DMA((n_scene // 2,)),
            pltpu.SemaphoreType.DMA((n_scene // 2,)),
            pltpu.SemaphoreType.DMA((n_seg,)),
            pltpu.SemaphoreType.DMA((n_seg,)),
        ],
        compiler_params=pltpu.CompilerParams(
            collective_id=0, has_side_effects=True, vmem_limit_bytes=VMEM_LIMIT),
    )(image, weight, column)


def normed(values, gain):
    center = values - jnp.mean(values, axis=-1, keepdims=True)
    spread = jnp.mean(center * center, axis=-1, keepdims=True)
    return (center * lax.rsqrt(spread + EPS) * gain).astype(BF16)


def gelu(values):
    return (0.5 * values * (1.0 + lax.erf(values * (0.5**0.5)))).astype(BF16)


def layer_patch(x, gain, w_in, w_out, w_up, w_down, query, key, value_t, mixed_t):
    width = x.shape[1]
    heads = width // HEAD_DIM
    normal = normed(x[...], gain[0:1, :])
    query[...] = (mm(normal, w_in[:, :width]) * (HEAD_DIM**-0.5 * LOG2E)).astype(BF16)
    key[...] = mm(normal, w_in[:, width:2 * width]).astype(BF16)
    value_t[...] = mm(normal, w_in[:, 2 * width:]).astype(BF16).T
    lane = lax.broadcasted_iota(I32, (PATCH, 128), 1) // HEAD_DIM

    def scores(i):
        group, head = i // 8, i % 8
        q = query[:, group * 128:(group + 1) * 128]
        q = jnp.where(lane == head, q, jnp.zeros((), BF16))
        k = key[:, group * 128:(group + 1) * 128]
        return lax.dot_general(q, k, NT, preferred_element_type=F32)

    def rest(i, score):
        raised = jnp.exp2(score - jnp.max(score, axis=1, keepdims=True)).astype(BF16)
        at = i * HEAD_DIM
        v = jnp.concatenate([value_t[at:at + HEAD_DIM, :], jnp.ones((16, PATCH), BF16)], axis=0)
        o = lax.dot_general(v, raised, NT, preferred_element_type=F32)
        mixed_t[at:at + HEAD_DIM, :] = (o[:HEAD_DIM] / o[HEAD_DIM:HEAD_DIM + 1]).astype(BF16)

    score = scores(0)
    for i in range(heads):
        following = scores(i + 1) if i + 1 < heads else None
        rest(i, score)
        score = following
    after = x[...] + mm(mixed_t[...].T, w_out[...])
    normal = normed(after, gain[1:2, :])
    hidden = w_up.shape[1]
    chunk = 512
    total = after
    up = mm(normal, w_up[:, :chunk])
    for at in range(0, hidden, chunk):
        following = mm(normal, w_up[:, at + chunk:at + 2 * chunk]) if at + chunk < hidden else None
        total = total + mm(gelu(up), w_down[at:at + chunk, :])
        up = following
    return total


def layers_kernel(n_seg, image_count, order_ref, inverse_ref, points_ref, image_row_ref, table_ref, gain_ref,
                  in_hbm, out_hbm, up_hbm, down_hbm, result_ref,
                  w_in, w_out, w_up, w_down, x, query, key, value_t, mixed_t,
                  send1, recv1, send2, recv2, wsem, ssem1, rsem1, ssem2, rsem2):
    scene = lax.axis_index("scene")
    me = lax.axis_index("seg")
    blocks = points_ref.shape[0]
    size = points_ref.shape[1]
    width = points_ref.shape[2]
    per = PATCH // size
    patches = blocks // per
    barrier = pltpu.get_barrier_semaphore()
    for k in range(1, n_seg):
        pl.semaphore_signal(barrier, inc=1, device_id=(scene, (me + k) % n_seg), device_id_type=MESH)
    loads = [
        [pltpu.make_async_copy(src.at[layer], dst.at[layer], wsem.at[layer, j])
         for j, (src, dst) in enumerate(((in_hbm, w_in), (out_hbm, w_out), (up_hbm, w_up), (down_hbm, w_down)))]
        for layer in range(2)
    ]
    for layer in range(2):
        for load in loads[layer]:
            load.start()
    for load in loads[0]:
        load.wait()
    pl.semaphore_wait(barrier, n_seg - 1)

    def piece(ref, patch, device):
        return ref.at[pl.ds((patch * n_seg + device) * per, per)]

    def copy1(patch, k):
        to = (me + k) % n_seg
        return pltpu.make_async_remote_copy(
            piece(send1, patch, to), piece(recv1, patch, me), ssem1.at[patch, k], rsem1.at[patch, k],
            device_id=(scene, to), device_id_type=MESH)

    def copy2(patch, k):
        to = (me + k) % n_seg
        return pltpu.make_async_remote_copy(
            piece(send2, patch, to), piece(recv2, patch, me), ssem2.at[patch, k], rsem2.at[patch, k],
            device_id=(scene, to), device_id_type=MESH)

    ORDER = [1, 4, 3, 12, 5, 15, 13, 7, 2, 8, 6, 9, 11, 14, 10]

    def compute(layer):
        return layer_patch(x, gain_ref.at[layer], w_in.at[layer], w_out.at[layer], w_up.at[layer],
                           w_down.at[layer], query, key, value_t, mixed_t)

    columns = width // COLS

    def first_patch(patch, carry):
        for b in range(per):
            block = lax.rem(order_ref[patch * per + b], blocks)
            row = image_row_ref[block]
            entry = lax.shift_right_logical(row, 11) * image_count + (row & (image_count - 1))
            count = table_ref.shape[0]
            hot = lax.broadcasted_iota(I32, (size, count), 1) == entry
            looked = mm(jnp.where(hot, 1.0, 0.0).astype(BF16), table_ref[...])
            x[b * size:(b + 1) * size, :] = points_ref[block].astype(F32) + looked
        out = compute(0).astype(BF16)
        for b in range(per):
            for r in range(size // ROWS):
                for c in range(columns):
                    send1[(patch * n_seg + r * columns + c) * per + b] = (
                        out[b * size + r * ROWS:b * size + (r + 1) * ROWS, c * COLS:(c + 1) * COLS])
        for k in ORDER:
            copy1(patch, k).start()
        for b in range(per):
            recv1[(patch * n_seg + me) * per + b] = send1[(patch * n_seg + me) * per + b]
        return carry

    lax.fori_loop(0, patches, first_patch, 0)
    for patch in range(patches):
        for k in ORDER:
            copy1(patch, k).wait_recv()
    for patch in range(patches):
        def fill(device, carry):
            for s in range(per):
                t = device * blocks + patch * per + s
                send2[(patch * n_seg + device) * per + s] = recv1[inverse_ref[t // 128, t % 128]]
            return carry

        lax.fori_loop(0, n_seg, fill, 0)
        for k in ORDER:
            copy2(patch, k).start()
        for s in range(per):
            recv2[(patch * n_seg + me) * per + s] = send2[(patch * n_seg + me) * per + s]
    for load in loads[1]:
        load.wait()

    def second_patch(patch, carry):
        for k in ORDER:
            copy2(patch, k).wait_recv()
        for s in range(per):
            for r in range(size // ROWS):
                for c in range(columns):
                    x[s * size + r * ROWS:s * size + (r + 1) * ROWS, c * COLS:(c + 1) * COLS] = (
                        recv2[(patch * n_seg + r * columns + c) * per + s].astype(F32))
        result_ref[pl.ds(patch * PATCH, PATCH), :] = compute(1).astype(BF16)
        return carry

    lax.fori_loop(0, patches, second_patch, 0)
    for patch in range(patches):
        for k in ORDER:
            copy1(patch, k).wait_send()
            copy2(patch, k).wait_send()


def layers_stage(n_seg, image_count, order, inverse, points, image_row, table, gain, w_in, w_out, w_up, w_down):
    length, width = points.shape
    blocks = order.shape[0]
    size = length // blocks
    patches = length // PATCH
    whole = pl.BlockSpec(memory_space=pltpu.VMEM)
    scalar = pl.BlockSpec(memory_space=pltpu.SMEM)
    hbm = pl.BlockSpec(memory_space=pl.ANY)
    pieces = (length // ROWS * (width // COLS), ROWS, COLS)
    dma = pltpu.SemaphoreType.DMA
    return pl.pallas_call(
        functools.partial(layers_kernel, n_seg, image_count),
        out_shape=jax.ShapeDtypeStruct((length, width), BF16),
        in_specs=[scalar, scalar, whole, whole, whole, whole, hbm, hbm, hbm, hbm],
        out_specs=whole,
        scratch_shapes=[
            pltpu.VMEM(w_in.shape, BF16),
            pltpu.VMEM(w_out.shape, BF16),
            pltpu.VMEM(w_up.shape, BF16),
            pltpu.VMEM(w_down.shape, BF16),
            pltpu.VMEM((PATCH, width), F32),
            pltpu.VMEM((PATCH, width), BF16),
            pltpu.VMEM((PATCH, width), BF16),
            pltpu.VMEM((width, PATCH), BF16),
            pltpu.VMEM((width, PATCH), BF16),
            pltpu.VMEM(pieces, BF16),
            pltpu.VMEM(pieces, BF16),
            pltpu.VMEM(pieces, BF16),
            pltpu.VMEM(pieces, BF16),
            dma((2, 4)),
            dma((patches, n_seg)),
            dma((patches, n_seg)),
            dma((patches, n_seg)),
            dma((patches, n_seg)),
        ],
        compiler_params=pltpu.CompilerParams(
            collective_id=1, has_side_effects=True, vmem_limit_bytes=VMEM_LIMIT),
    )(order, inverse, points.reshape(blocks, size, width), image_row.reshape(blocks, size, 1), table, gain,
      w_in, w_out, w_up, w_down)


def local(n_scene, n_seg, points, zorder, image, image_row, image_weight, norm_gain, in_weight, out_weight,
          up_weight, down_weight, hilbert_target):
    table, inverse = image_stage(image, image_weight, hilbert_target, n_scene, n_seg)
    return layers_stage(n_seg, image.shape[0], zorder, inverse, points, image_row, table, norm_gain,
                        in_weight, out_weight, up_weight, down_weight)


def solution(mesh):
    placed = (
        P(("scene", "seg"), None),
        P(("scene", "seg")),
        P(("scene", "seg"), None),
        P(("scene", "seg")),
        P(),
        P(),
        P(),
        P(),
        P(),
        P(),
        P(("scene", "seg")),
    )
    return jax.shard_map(
        functools.partial(local, mesh.shape["scene"], mesh.shape["seg"]),
        mesh=mesh, in_specs=placed, out_specs=P(("scene", "seg"), None), check_vma=False)
```

profile of v0, /device:TPU:1, one launch (start us, length us, event | category | flops | bytes accessed | tf_op | source)
XLA Modules:
  0.0 137.6 jit_solution(1388908645734364261)
XLA Ops:
  0.0 0.7 pad.4
  0.7 0.7 broadcast_in_dim.2.target_ref
  1.3 1.9 %copy.12.image_row_ref = s32[12,128,1]{2,1,0:T(8,128)} copy(s32[12,128,1]{1,0,2:T(8,128)} %bitcast.3) | data formatting | bytes 12288 | tf_op jit(solution)/shard_map/reshape | solution.py:312
  3.2 20.8 %shard_map.109 = (bf16[1024,512]{1,0:T(8,128)(2,1)}, s32[2,128]{1,0:T(2,128)}) custom-call(bf16[128,1024]{1,0:T(8,128)(2,1)} %image_ref.1, bf16[1024,512]{1,0:T(8,128)(2,1)} %weight_ref.1, s32[16,128]{1,0:T(8,128)} %broadcast_in_dim.2.target_ref), custom_call_target="tpu_custom_call" | custom-call | tf_op jit(solution)/shard_map/pallas_call | solution.py:97
  24.0 110.9 %shard_map.110 = bf16[1536,512]{1,0:T(8,128)(2,1)} custom-call(s32[12]{0:T(128)} %order_ref.1, s32[2,128]{1,0:T(2,128)} %get-tuple-element.7.inverse_ref, bf16[12,128,512]{2,1,0:T(8,128)(2,1)} %bitcast.2, s32[12,128,1]{2,1,0:T(8,128)} %copy.12.image_row_ref, bf16[1024,512]{1,0:T(8,128)(2,1)} %get-tuple-element.8.table_ref, f32[2,2,512]{2,1,0:T(2,128)} %gain_ref.1, ...), custom_call_target="tpu_custom_call" | custom-call | tf_op jit(solution)/shard_map/pallas_call | solution.py:285
  135.0 2.7 %copy.14 = bf16[1536,512]{1,0:T(8,128)(2,1)} copy(bf16[1536,512]{1,0:T(8,128)(2,1)} %shard_map.110) | data formatting | bytes 3145728
where the time goes:
time: 139 us; the launch traced here: 138 us
  Pallas kernels  132 us (95%)
  local copies, waits for them, and re-layouts  5.84 us (4%)
    pallas_call x1, Pallas kernels, layers_stage(): pl.pallas_call(functools.partial(layers_kernel, n_seg, image_count), out_...  111 us
    pallas_call x1, Pallas kernels, image_stage(): pl.pallas_call(functools.partial(image_kernel, n_scene, n_seg, blocks), o...  20.8 us

commit v1 on v0

v1 whole, which is shorter than its diff:
```python
import functools

import jax
import jax.numpy as jnp
from jax import lax
from jax.experimental import pallas as pl
from jax.experimental.pallas import tpu as pltpu
from jax.sharding import PartitionSpec as P

HEAD_DIM = 16
PATCH = 512
EPS = 1e-05
LOG2E = 1.4426950408889634
MESH = pl.DeviceIdType.MESH
F32, BF16, I32 = jnp.float32, jnp.bfloat16, jnp.int32
NT = (((1,), (1,)), ((), ()))
ROWS, COLS = 16, 256
VMEM_LIMIT = 60 * 2**20


def mm(a, b):
    return jnp.dot(a, b, preferred_element_type=F32)


def normed(values, gain):
    center = values - jnp.mean(values, axis=-1, keepdims=True)
    spread = jnp.mean(center * center, axis=-1, keepdims=True)
    return (center * lax.rsqrt(spread + EPS) * gain).astype(BF16)


def gelu(values):
    return (0.5 * values * (1.0 + lax.erf(values * (0.5**0.5)))).astype(BF16)


def layer_patch(x, gain, w_in, w_out, w_up, w_down, query, key, value_t, mixed_t):
    width = x.shape[1]
    heads = width // HEAD_DIM
    normal = normed(x[...], gain[0:1, :])
    query[...] = (mm(normal, w_in[:, :width]) * (HEAD_DIM**-0.5 * LOG2E)).astype(BF16)
    key[...] = mm(normal, w_in[:, width:2 * width]).astype(BF16)
    value_t[...] = mm(normal, w_in[:, 2 * width:]).astype(BF16).T
    lane = lax.broadcasted_iota(I32, (PATCH, 128), 1) // HEAD_DIM

    def scores(i):
        group, head = i // 8, i % 8
        q = query[:, group * 128:(group + 1) * 128]
        q = jnp.where(lane == head, q, jnp.zeros((), BF16))
        k = key[:, group * 128:(group + 1) * 128]
        return lax.dot_general(q, k, NT, preferred_element_type=F32)

    def raised(score):
        return jnp.exp2(score - jnp.max(score, axis=1, keepdims=True)).astype(BF16)

    def mix(i, weights):
        at = i * HEAD_DIM
        v = jnp.concatenate([value_t[at:at + HEAD_DIM, :], jnp.ones((16, PATCH), BF16)], axis=0)
        o = lax.dot_general(v, weights, NT, preferred_element_type=F32)
        mixed_t[at:at + HEAD_DIM, :] = (o[:HEAD_DIM] / o[HEAD_DIM:HEAD_DIM + 1]).astype(BF16)

    score, weights = scores(0), None
    for i in range(heads):
        following = scores(i + 1) if i + 1 < heads else None
        exponents = raised(score)
        if i > 0:
            mix(i - 1, weights)
        score, weights = following, exponents
    mix(heads - 1, weights)
    after = x[...] + mm(mixed_t[...].T, w_out[...])
    normal = normed(after, gain[1:2, :])
    hidden = w_up.shape[1]
    chunk = 512
    total = after
    up = mm(normal, w_up[:, :chunk])
    for at in range(0, hidden, chunk):
        following = mm(normal, w_up[:, at + chunk:at + 2 * chunk]) if at + chunk < hidden else None
        total = total + mm(gelu(up), w_down[at:at + chunk, :])
        up = following
    return total


ORDER = (1, 4, 3, 12, 5, 15, 13, 7, 2, 8, 6, 9, 11, 14, 10)


def kernel(n_scene, n_seg, order_ref, target_ref, gain_ref, image_row_ref,
           image_hbm, weight_hbm, points_hbm, in_hbm, out_hbm, up_hbm, down_hbm, result_ref,
           image, image_weight, points, w_in, w_out, w_up, w_down,
           table, targets, inverse_v, inverse, x, query, key, value_t, mixed_t,
           send1, recv1, send2, recv2,
           wsem, psem, isem, asend, arecv, fsend, frecv, tsend, trecv, ssem1, rsem1, ssem2, rsem2):
    scene = lax.axis_index("scene")
    me = lax.axis_index("seg")
    blocks, size, width = points.shape
    per = PATCH // size
    patches = blocks // per
    columns = width // COLS
    count = image.shape[0]
    side = 4
    core = scene % 2
    level = scene // 2
    chips = n_scene // 2
    other = level * 2 + 1 - core

    def peer(k):
        return (me // side + k // side) % side * side + (me + k) % side

    barrier = pltpu.get_barrier_semaphore()
    for k in range(1, chips):
        pl.semaphore_signal(barrier, inc=1, device_id=((level + k) % chips * 2 + core, me), device_id_type=MESH)
    pl.semaphore_signal(barrier, inc=1, device_id=(other, me), device_id_type=MESH)
    for k in range(1, n_seg):
        pl.semaphore_signal(barrier, inc=1, device_id=(scene, peer(k)), device_id_type=MESH)

    first = [pltpu.make_async_copy(image_hbm, image, isem.at[0]),
             pltpu.make_async_copy(weight_hbm, image_weight, isem.at[1])]
    load_points = pltpu.make_async_copy(points_hbm, points, psem.at[0])
    loads = [
        [pltpu.make_async_copy(src.at[layer], dst.at[layer], wsem.at[layer, j])
         for j, (src, dst) in enumerate(((in_hbm, w_in), (out_hbm, w_out), (up_hbm, w_up), (down_hbm, w_down)))]
        for layer in range(2)
    ]
    for load in first + [load_points] + loads[0] + loads[1]:
        load.start()

    sublane = lax.broadcasted_iota(I32, (16, 128), 0)
    column = jnp.full((16, 128), -1, I32)
    for j in range(blocks):
        column = jnp.where(sublane == j, target_ref[j], column)
    targets[me] = column
    for load in first:
        load.wait()
    table[scene] = mm(image[...], image_weight[...]).astype(BF16)
    pl.semaphore_wait(barrier, chips + n_seg - 1)

    def across(k):
        return pltpu.make_async_remote_copy(
            table.at[scene], table.at[scene], asend.at[k], arecv.at[k],
            device_id=((level + k) % chips * 2 + core, me), device_id_type=MESH)

    def forward(k):
        held = (level + chips - k) % chips * 2 + core
        return pltpu.make_async_remote_copy(
            table.at[held], table.at[held], fsend.at[k], frecv.at[k],
            device_id=(other, me), device_id_type=MESH)

    def tell(k):
        return pltpu.make_async_remote_copy(
            targets.at[me], targets.at[me], tsend.at[k], trecv.at[k],
            device_id=(scene, peer(k)), device_id_type=MESH)

    hops = [k for k in (1, chips - 1, 2)]
    for k in hops:
        across(k).start()
    forward(0).start()
    for k in ORDER:
        tell(k).start()
    for k in hops[:2]:
        across(k).wait_recv()
        forward(k).start()
    for k in ORDER:
        tell(k).wait_recv()
    base = scene * (n_seg * blocks)
    lane = lax.broadcasted_iota(I32, (16, 128), 1)
    within = sublane // per * (n_seg * per) + sublane % per
    for part in range(2):
        total = jnp.zeros((16, 128), I32)
        for source in range(n_seg):
            hit = targets[source] == lane + (base + part * 128)
            total = total + jnp.where(hit, within + source * per, 0)
        summed = total[:8] + total[8:]
        for step in (4, 2, 1):
            summed = summed[:step] + summed[step:]
        summed = jnp.minimum(summed, n_seg * blocks - 1)
        inverse_v[part * 8:(part + 1) * 8, :] = jnp.broadcast_to(summed, (8, 128))
    to_scalars = pltpu.make_async_copy(inverse_v, inverse, isem.at[2])
    to_scalars.start()
    across(2).wait_recv()
    forward(2).start()
    row = image_row_ref[...]
    entry = lax.shift_right_logical(row, 11) * count + (row & (count - 1))
    entry = jnp.concatenate([entry, jnp.zeros((16 - blocks, size), I32)], axis=0).astype(F32).T
    pick = lax.broadcasted_iota(I32, (size, 16), 1)
    rows = lax.broadcasted_iota(I32, (size, n_scene * count), 1)
    load_points.wait()
    for load in loads[0]:
        load.wait()
    for k in range(chips):
        forward(k).wait_recv()
    to_scalars.wait()

    def piece(ref, patch, device):
        return ref.at[pl.ds((patch * n_seg + device) * per, per)]

    def copy1(patch, k):
        return pltpu.make_async_remote_copy(
            piece(send1, patch, peer(k)), piece(recv1, patch, me), ssem1.at[patch, k], rsem1.at[patch, k],
            device_id=(scene, peer(k)), device_id_type=MESH)

    def copy2(patch, k):
        return pltpu.make_async_remote_copy(
            piece(send2, patch, peer(k)), piece(recv2, patch, me), ssem2.at[patch, k], rsem2.at[patch, k],
            device_id=(scene, peer(k)), device_id_type=MESH)

    def compute(layer):
        return layer_patch(x, gain_ref.at[layer], w_in.at[layer], w_out.at[layer], w_up.at[layer],
                           w_down.at[layer], query, key, value_t, mixed_t)

    def first_patch(patch, carry):
        for b in range(per):
            block = lax.rem(order_ref[patch * per + b], blocks)
            mine = jnp.sum(jnp.where(pick == block, entry, 0.0), axis=1, keepdims=True).astype(I32)
            hot = jnp.where(rows == mine, 1.0, 0.0).astype(BF16)
            looked = mm(hot, table[...].reshape(n_scene * count, width))
            x[b * size:(b + 1) * size, :] = points[block].astype(F32) + looked
        out = compute(0).astype(BF16)
        for b in range(per):
            for r in range(size // ROWS):
                for c in range(columns):
                    send1[(patch * n_seg + r * columns + c) * per + b] = (
                        out[b * size + r * ROWS:b * size + (r + 1) * ROWS, c * COLS:(c + 1) * COLS])
        for k in ORDER:
            copy1(patch, k).start()
        for b in range(per):
            recv1[(patch * n_seg + me) * per + b] = send1[(patch * n_seg + me) * per + b]
        return carry

    lax.fori_loop(0, patches, first_patch, 0)
    for patch in range(patches):
        for k in ORDER:
            copy1(patch, k).wait_recv()

    def send_patch(patch):
        for k in ORDER:
            copy2(patch, k).start()

    for patch in range(patches):
        def fill(device, carry):
            for s in range(per):
                t = device * blocks + patch * per + s
                send2[(patch * n_seg + device) * per + s] = recv1[inverse[t // 128 * 8, t % 128]]
            return carry

        lax.fori_loop(0, n_seg, fill, 0)
        if patch == 0:
            send_patch(0)
        for s in range(per):
            recv2[(patch * n_seg + me) * per + s] = send2[(patch * n_seg + me) * per + s]
    for load in loads[1]:
        load.wait()

    def second_patch(patch, carry):
        for k in ORDER:
            copy2(patch, k).wait_recv()

        @pl.when(patch + 1 < patches)
        def _():
            send_patch(patch + 1)

        for s in range(per):
            for r in range(size // ROWS):
                for c in range(columns):
                    x[s * size + r * ROWS:s * size + (r + 1) * ROWS, c * COLS:(c + 1) * COLS] = (
                        recv2[(patch * n_seg + r * columns + c) * per + s].astype(F32))
        result_ref[pl.ds(patch * PATCH, PATCH), :] = compute(1).astype(BF16)
        return carry

    lax.fori_loop(0, patches, second_patch, 0)
    for k in hops:
        across(k).wait_send()
    for k in range(chips):
        forward(k).wait_send()
    for k in ORDER:
        tell(k).wait_send()
    for patch in range(patches):
        for k in ORDER:
            copy1(patch, k).wait_send()
            copy2(patch, k).wait_send()


def local(n_scene, n_seg, points, zorder, image, image_row, image_weight, norm_gain, in_weight, out_weight,
          up_weight, down_weight, hilbert_target):
    length, width = points.shape
    blocks = zorder.shape[0]
    size = length // blocks
    patches = length // PATCH
    count = image.shape[0]
    chips = n_scene // 2
    whole = pl.BlockSpec(memory_space=pltpu.VMEM)
    scalar = pl.BlockSpec(memory_space=pltpu.SMEM)
    hbm = pl.BlockSpec(memory_space=pl.ANY)
    pieces = (length // ROWS * (width // COLS), ROWS, COLS)
    dma = pltpu.SemaphoreType.DMA
    return pl.pallas_call(
        functools.partial(kernel, n_scene, n_seg),
        out_shape=jax.ShapeDtypeStruct((length, width), BF16),
        in_specs=[scalar, scalar, whole, whole] + [hbm] * 7,
        out_specs=whole,
        scratch_shapes=[
            pltpu.VMEM(image.shape, BF16),
            pltpu.VMEM(image_weight.shape, BF16),
            pltpu.VMEM((blocks, size, width), BF16),
            pltpu.VMEM(in_weight.shape, BF16),
            pltpu.VMEM(out_weight.shape, BF16),
            pltpu.VMEM(up_weight.shape, BF16),
            pltpu.VMEM(down_weight.shape, BF16),
            pltpu.VMEM((n_scene, count, width), BF16),
            pltpu.VMEM((n_seg, 16, 128), I32),
            pltpu.VMEM((16, 128), I32),
            pltpu.SMEM((16, 128), I32),
            pltpu.VMEM((PATCH, width), F32),
            pltpu.VMEM((PATCH, width), BF16),
            pltpu.VMEM((PATCH, width), BF16),
            pltpu.VMEM((width, PATCH), BF16),
            pltpu.VMEM((width, PATCH), BF16),
            pltpu.VMEM(pieces, BF16),
            pltpu.VMEM(pieces, BF16),
            pltpu.VMEM(pieces, BF16),
            pltpu.VMEM(pieces, BF16),
            dma((2, 4)),
            dma((1,)),
            dma((3,)),
            dma((chips,)),
            dma((chips,)),
            dma((chips,)),
            dma((chips,)),
            dma((n_seg,)),
            dma((n_seg,)),
            dma((patches, n_seg)),
            dma((patches, n_seg)),
            dma((patches, n_seg)),
            dma((patches, n_seg)),
        ],
        compiler_params=pltpu.CompilerParams(
            collective_id=0, has_side_effects=True, vmem_limit_bytes=VMEM_LIMIT),
    )(zorder, hilbert_target, norm_gain, image_row.reshape(blocks, size), image, image_weight,
      points.reshape(blocks, size, width), in_weight, out_weight, up_weight, down_weight)


def solution(mesh):
    placed = (
        P(("scene", "seg"), None),
        P(("scene", "seg")),
        P(("scene", "seg"), None),
        P(("scene", "seg")),
        P(),
        P(),
        P(),
        P(),
        P(),
        P(),
        P(("scene", "seg")),
    )
    return jax.shard_map(
        functools.partial(local, mesh.shape["scene"], mesh.shape["seg"]),
        mesh=mesh, in_specs=placed, out_specs=P(("scene", "seg"), None), check_vma=False)
```

time: 139 us -> 127 us (0.914)
  Pallas kernels: 132 us -> 124 us
  local copies, waits for them, and re-layouts: 5.84 us -> 2.65 us
    pallas_call x2 -> x1, Pallas kernels: 132 us -> 124 us  [local(): pl.pallas_call(functools.partial(kernel, n_scene, n_seg), out_shape=jax.S...]
    reshape x1 -> x0, local copies, waits for them, and re-layouts: 1.87 us -> none  [layers_stage(): image_row.reshape(blocks, size, 1)]
where the time goes in v1:
time: 127 us; the launch traced here: 126 us
  Pallas kernels  124 us (98%)
  local copies, waits for them, and re-layouts  2.65 us (2%)
    pallas_call x1, Pallas kernels, local(): pl.pallas_call(functools.partial(kernel, n_scene, n_seg), out_shape=jax.S...  124 us
    unnamed x1, local copies, waits for them, and re-layouts  2.65 us

profile of v1, /device:TPU:1, one launch (start us, length us, event | category | flops | bytes accessed | tf_op | source)
XLA Modules:
  0.0 126.5 jit_solution(8380738490346671581)
XLA Ops:
  0.0 123.8 %shard_map.109 = bf16[1536,512]{1,0:T(8,128)(2,1)} custom-call(s32[12]{0:T(128)} %order_ref.1, s32[12]{0:T(128)} %target_ref.1, f32[2,2,512]{2,1,0:T(2,128)} %gain_ref.1, s32[12,128]{1,0:T(8,128)} %bitcast.3, bf16[128,1024]{1,0:T(8,128)(2,1)} %image_hbm.1, bf16[1024,512]{1,0:T(8,128)(2,1)} %weight_hbm.1, bf16[12,128,512]{2,1,0:T(8,128)(2,1)} %bitcast.2, ...), custom_call_target="tpu_custom_call" | custom-call | tf_op jit(solution)/shard_map/pallas_call | solution.py:292
  123.8 2.7 %copy.13 = bf16[1536,512]{1,0:T(8,128)(2,1)} copy(bf16[1536,512]{1,0:T(8,128)(2,1)} %shard_map.109) | data formatting | bytes 3145728

commit v2 on v1

--- a/solution.py
+++ b/solution.py
@@ -15,7 +15,7 @@
 F32, BF16, I32 = jnp.float32, jnp.bfloat16, jnp.int32
 NT = (((1,), (1,)), ((), ()))
 ROWS, COLS = 16, 256
-VMEM_LIMIT = 60 * 2**20
+VMEM_LIMIT = 61 * 2**20
 
 
 def mm(a, b):
@@ -32,18 +32,20 @@
     return (0.5 * values * (1.0 + lax.erf(values * (0.5**0.5)))).astype(BF16)
 
 
-def layer_patch(x, gain, w_in, w_out, w_up, w_down, query, key, value_t, mixed_t):
+def layer_patch(x, gain, w_in, w_out, w_up, w_down, query, key, value_t, mixed_t, parts, emit):
     width = x.shape[1]
     heads = width // HEAD_DIM
     normal = normed(x[...], gain[0:1, :])
     query[...] = (mm(normal, w_in[:, :width]) * (HEAD_DIM**-0.5 * LOG2E)).astype(BF16)
     key[...] = mm(normal, w_in[:, width:2 * width]).astype(BF16)
     value_t[...] = mm(normal, w_in[:, 2 * width:]).astype(BF16).T
-    lane = lax.broadcasted_iota(I32, (PATCH, 128), 1) // HEAD_DIM
-
-    def scores(i):
+    half = 256
+    lane = lax.broadcasted_iota(I32, (half, 128), 1) // HEAD_DIM
+
+    def scores(step):
+        part, i = step
         group, head = i // 8, i % 8
-        q = query[:, group * 128:(group + 1) * 128]
+        q = query[part * half:(part + 1) * half, group * 128:(group + 1) * 128]
         q = jnp.where(lane == head, q, jnp.zeros((), BF16))
         k = key[:, group * 128:(group + 1) * 128]
         return lax.dot_general(q, k, NT, preferred_element_type=F32)
@@ -51,31 +53,45 @@
     def raised(score):
         return jnp.exp2(score - jnp.max(score, axis=1, keepdims=True)).astype(BF16)
 
-    def mix(i, weights):
+    def mix(step, weights):
+        part, i = step
         at = i * HEAD_DIM
         v = jnp.concatenate([value_t[at:at + HEAD_DIM, :], jnp.ones((16, PATCH), BF16)], axis=0)
         o = lax.dot_general(v, weights, NT, preferred_element_type=F32)
-        mixed_t[at:at + HEAD_DIM, :] = (o[:HEAD_DIM] / o[HEAD_DIM:HEAD_DIM + 1]).astype(BF16)
-
-    score, weights = scores(0), None
-    for i in range(heads):
-        following = scores(i + 1) if i + 1 < heads else None
-        exponents = raised(score)
-        if i > 0:
-            mix(i - 1, weights)
-        score, weights = following, exponents
-    mix(heads - 1, weights)
-    after = x[...] + mm(mixed_t[...].T, w_out[...])
-    normal = normed(after, gain[1:2, :])
-    hidden = w_up.shape[1]
-    chunk = 512
-    total = after
-    up = mm(normal, w_up[:, :chunk])
-    for at in range(0, hidden, chunk):
-        following = mm(normal, w_up[:, at + chunk:at + 2 * chunk]) if at + chunk < hidden else None
-        total = total + mm(gelu(up), w_down[at:at + chunk, :])
-        up = following
-    return total
+        mixed_t[at:at + HEAD_DIM, part * half:(part + 1) * half] = (
+            o[:HEAD_DIM] / o[HEAD_DIM:HEAD_DIM + 1]).astype(BF16)
+
+    def finish(part, rows):
+        at = slice(part * rows, (part + 1) * rows)
+        after = x[at, :] + mm(mixed_t[:, at].T, w_out[...])
+        normal = normed(after, gain[1:2, :])
+        hidden = w_up.shape[1]
+        chunk = 512
+        total = after
+        up = mm(normal, w_up[:, :chunk])
+        for at in range(0, hidden, chunk):
+            following = mm(normal, w_up[:, at + chunk:at + 2 * chunk]) if at + chunk < hidden else None
+            total = total + mm(gelu(up), w_down[at:at + chunk, :])
+            up = following
+        emit(part, total)
+
+    steps = [(part, i) for part in range(PATCH // half) for i in range(heads)]
+    lead, lag = 2, 2
+    score = {n: scores(steps[n]) for n in range(lead)}
+    weights = {}
+    for n in range(len(steps) + lag):
+        if n + lead < len(steps):
+            score[n + lead] = scores(steps[n + lead])
+        if n < len(steps):
+            weights[n] = raised(score.pop(n))
+        if n >= lag:
+            mix(steps[n - lag], weights.pop(n - lag))
+            if parts > 1 and n - lag + 1 == heads:
+                finish(0, half)
+    if parts > 1:
+        finish(1, half)
+    else:
+        finish(0, PATCH)
 
 
 ORDER = (1, 4, 3, 12, 5, 15, 13, 7, 2, 8, 6, 9, 11, 14, 10)
@@ -84,7 +100,7 @@
 def kernel(n_scene, n_seg, order_ref, target_ref, gain_ref, image_row_ref,
            image_hbm, weight_hbm, points_hbm, in_hbm, out_hbm, up_hbm, down_hbm, result_ref,
            image, image_weight, points, w_in, w_out, w_up, w_down,
-           table, targets, inverse_v, inverse, x, query, key, value_t, mixed_t,
+           table, targets, inverse_v, inverse, hot, x, query, key, value_t, mixed_t,
            send1, recv1, send2, recv2,
            wsem, psem, isem, asend, arecv, fsend, frecv, tsend, trecv, ssem1, rsem1, ssem2, rsem2):
     scene = lax.axis_index("scene")
@@ -180,6 +196,10 @@
     entry = jnp.concatenate([entry, jnp.zeros((16 - blocks, size), I32)], axis=0).astype(F32).T
     pick = lax.broadcasted_iota(I32, (size, 16), 1)
     rows = lax.broadcasted_iota(I32, (size, n_scene * count), 1)
+    for b in range(blocks):
+        block = lax.rem(order_ref[b], blocks)
+        mine = jnp.sum(jnp.where(pick == block, entry, 0.0), axis=1, keepdims=True).astype(I32)
+        hot[b * size:(b + 1) * size, :] = jnp.where(rows == mine, 1.0, 0.0).astype(BF16)
     load_points.wait()
     for load in loads[0]:
         load.wait()
@@ -190,9 +210,12 @@
     def piece(ref, patch, device):
         return ref.at[pl.ds((patch * n_seg + device) * per, per)]
 
-    def copy1(patch, k):
-        return pltpu.make_async_remote_copy(
-            piece(send1, patch, peer(k)), piece(recv1, patch, me), ssem1.at[patch, k], rsem1.at[patch, k],
+    def copy1(patch, part, k):
+        ranks = per // 2
+        there = pl.ds((patch * n_seg + peer(k)) * per + part * ranks, ranks)
+        here = pl.ds((patch * n_seg + me) * per + part * ranks, ranks)
+        return pltpu.make_async_remote_copy(
+            send1.at[there], recv1.at[here], ssem1.at[patch * 2 + part, k], rsem1.at[patch * 2 + part, k],
             device_id=(scene, peer(k)), device_id_type=MESH)
 
     def copy2(patch, k):
@@ -200,33 +223,38 @@
             piece(send2, patch, peer(k)), piece(recv2, patch, me), ssem2.at[patch, k], rsem2.at[patch, k],
             device_id=(scene, peer(k)), device_id_type=MESH)
 
-    def compute(layer):
-        return layer_patch(x, gain_ref.at[layer], w_in.at[layer], w_out.at[layer], w_up.at[layer],
-                           w_down.at[layer], query, key, value_t, mixed_t)
+    def compute(layer, parts, emit):
+        layer_patch(x, gain_ref.at[layer], w_in.at[layer], w_out.at[layer], w_up.at[layer],
+                    w_down.at[layer], query, key, value_t, mixed_t, parts, emit)
 
     def first_patch(patch, carry):
+        at = pl.ds(patch * PATCH, PATCH)
+        x[...] = mm(hot[at, :], table[...].reshape(n_scene * count, width))
         for b in range(per):
             block = lax.rem(order_ref[patch * per + b], blocks)
-            mine = jnp.sum(jnp.where(pick == block, entry, 0.0), axis=1, keepdims=True).astype(I32)
-            hot = jnp.where(rows == mine, 1.0, 0.0).astype(BF16)
-            looked = mm(hot, table[...].reshape(n_scene * count, width))
-            x[b * size:(b + 1) * size, :] = points[block].astype(F32) + looked
-        out = compute(0).astype(BF16)
-        for b in range(per):
-            for r in range(size // ROWS):
-                for c in range(columns):
-                    send1[(patch * n_seg + r * columns + c) * per + b] = (
-                        out[b * size + r * ROWS:b * size + (r + 1) * ROWS, c * COLS:(c + 1) * COLS])
-        for k in ORDER:
-            copy1(patch, k).start()
+            x[b * size:(b + 1) * size, :] += points[block].astype(F32)
+
+        def emit(part, result):
+            out = result.astype(BF16)
+            for j in range(per // 2):
+                b = part * (per // 2) + j
+                for r in range(size // ROWS):
+                    for c in range(columns):
+                        send1[(patch * n_seg + r * columns + c) * per + b] = (
+                            out[j * size + r * ROWS:j * size + (r + 1) * ROWS, c * COLS:(c + 1) * COLS])
+            for k in ORDER:
+                copy1(patch, part, k).start()
+
+        compute(0, 2, emit)
         for b in range(per):
             recv1[(patch * n_seg + me) * per + b] = send1[(patch * n_seg + me) * per + b]
         return carry
 
     lax.fori_loop(0, patches, first_patch, 0)
     for patch in range(patches):
-        for k in ORDER:
-            copy1(patch, k).wait_recv()
+        for part in range(2):
+            for k in ORDER:
+                copy1(patch, part, k).wait_recv()
 
     def send_patch(patch):
         for k in ORDER:
@@ -260,7 +288,11 @@
                 for c in range(columns):
                     x[s * size + r * ROWS:s * size + (r + 1) * ROWS, c * COLS:(c + 1) * COLS] = (
                         recv2[(patch * n_seg + r * columns + c) * per + s].astype(F32))
-        result_ref[pl.ds(patch * PATCH, PATCH), :] = compute(1).astype(BF16)
+
+        def emit(part, result):
+            result_ref[pl.ds(patch * PATCH, PATCH), :] = result.astype(BF16)
+
+        compute(1, 1, emit)
         return carry
 
     lax.fori_loop(0, patches, second_patch, 0)
@@ -272,7 +304,8 @@
         tell(k).wait_send()
     for patch in range(patches):
         for k in ORDER:
-            copy1(patch, k).wait_send()
+            copy1(patch, 0, k).wait_send()
+            copy1(patch, 1, k).wait_send()
             copy2(patch, k).wait_send()
 
 
@@ -291,7 +324,7 @@
     dma = pltpu.SemaphoreType.DMA
     return pl.pallas_call(
         functools.partial(kernel, n_scene, n_seg),
-        out_shape=jax.ShapeDtypeStruct((length, width), BF16),
+        out_shape=pltpu.VMEM((length, width), BF16),
         in_specs=[scalar, scalar, whole, whole] + [hbm] * 7,
         out_specs=whole,
         scratch_shapes=[
@@ -306,6 +339,7 @@
             pltpu.VMEM((n_seg, 16, 128), I32),
             pltpu.VMEM((16, 128), I32),
             pltpu.SMEM((16, 128), I32),
+            pltpu.VMEM((length, n_scene * count), BF16),
             pltpu.VMEM((PATCH, width), F32),
             pltpu.VMEM((PATCH, width), BF16),
             pltpu.VMEM((PATCH, width), BF16),
@@ -324,8 +358,8 @@
             dma((chips,)),
             dma((n_seg,)),
             dma((n_seg,)),
-            dma((patches, n_seg)),
-            dma((patches, n_seg)),
+            dma((patches * 2, n_seg)),
+            dma((patches * 2, n_seg)),
             dma((patches, n_seg)),
             dma((patches, n_seg)),
         ],

time: 127 us -> 123 us (0.969)
  Pallas kernels: 124 us -> 122 us
  local copies, waits for them, and re-layouts: 2.65 us -> 1.15 us
    pallas_call x1, Pallas kernels: 124 us -> 122 us  [local(): pl.pallas_call(functools.partial(kernel, n_scene, n_seg), out_shape=pltpu...]
    unnamed x1, local copies, waits for them, and re-layouts: 2.65 us -> 1.15 us
where the time goes in v2:
time: 123 us
  Pallas kernels  122 us (99%)
    pallas_call x1, Pallas kernels, local(): pl.pallas_call(functools.partial(kernel, n_scene, n_seg), out_shape=pltpu...  122 us

profile of v2, /device:TPU:1, one launch (start us, length us, event | category | flops | bytes accessed | tf_op | source)
XLA Modules:
  0.0 123.0 jit_solution(15539445850532432884)
XLA Ops:
  0.0 121.9 %shard_map.109 = bf16[1536,512]{1,0:T(8,128)(2,1)S(1)} custom-call(s32[12]{0:T(128)} %order_ref.1, s32[12]{0:T(128)} %target_ref.1, f32[2,2,512]{2,1,0:T(2,128)} %gain_ref.1, s32[12,128]{1,0:T(8,128)} %bitcast.3, bf16[128,1024]{1,0:T(8,128)(2,1)} %image_hbm.1, bf16[1024,512]{1,0:T(8,128)(2,1)} %weight_hbm.1, bf16[12,128,512]{2,1,0:T(8,128)(2,1)} %bitcast.2, ...), custom_call_target="tpu_custom_call" | custom-call | tf_op jit(solution)/shard_map/pallas_call | solution.py:325
  121.9 1.1 copy.13
